TPU v7x, 256 devices: a whole 4x4x8 slice. The times are simulated.
256 devices in a mesh: elec: 32 (over z, y), cell: 8 (over x, core).
Axes of the slice: x: 4, y: 4, z: 8, core: 2. Of those that a mesh axis runs over, the one named last changes fastest.
Arguments:
- fields: bfloat16 [512, 3, 65536], P('elec', None, 'cell'), may hold values from -6 to 6
- cell_weight: float32 [65536], P('cell')
- resolution_basis: bfloat16 [65536, 512], P('cell')
- pattern: int32 [32, 4], P('elec'), may hold values from 0 to 1, as said below
- quadrupoles: int32 [2048, 4], P('elec'), may hold values from 0 to 511, as said below
Outputs:
- projection: float32 [512, 2048], P('cell', 'elec')
- design_gain: float32 [2048], P('elec')
Inputs may be any that keep to these rules, and one draw needn't show every extreme that they name: `pattern`: row i is 1 for offsets below a count of 1 to 4 and 0 from there on; the count never reaches past the last block (32 - i at most), and some row has 4 ones. `quadrupoles`: A, B, M, N are four different electrodes. A and B lie in one block of 16 electrodes (electrode // 16); M and N lie together in that block or one of the next 3 blocks, at an offset that pattern marks 1 for A's block. Among the 64 candidates of one device (aligned blocks of rows), at most 4 have A in any one block, and on every device some electrode block holds exactly 4 of them.
All inputs are finite; a program needn't handle non-finite values.
Results may differ from a plain program's by a relative error of at most 0.0029.
Values may be sent and summed in bfloat16 or wider, within the bound.
A program may use at most 128 MiB of HBM per device.

v0:
```python
import jax
import jax.numpy as jnp
from jax import lax
from jax.sharding import PartitionSpec as P


def from_behind(block, axis, distance):
    devices = range(lax.axis_size(axis))
    route = [(i - distance, i) for i in devices if i - distance in devices]
    return lax.ppermute(block, axis, route)


def pair_tile(own_fields, partner, cell_weight):
    left_wide = own_fields.astype(jnp.float32)
    right_wide = partner.astype(jnp.float32)
    summed = left_wide[:, None, 0, :] * right_wide[None, :, 0, :]
    summed = summed + left_wide[:, None, 1, :] * right_wide[None, :, 1, :]
    summed = summed + left_wide[:, None, 2, :] * right_wide[None, :, 2, :]
    number = own_fields.shape[0] * partner.shape[0]
    return (summed * cell_weight).astype(jnp.bfloat16).reshape(number, -1)


def per_device(fields, cell_weight, resolution_basis, pattern, quadrupoles):
    electrodes = fields.shape[0]
    square = electrodes * electrodes
    columns = resolution_basis.shape[1]
    reach_count = pattern.shape[1]
    live_tiles = pattern[0]
    partner_list = [fields]
    for offset in range(1, reach_count):
        partner_list.append(from_behind(fields, "elec", -offset))
    products = jnp.concatenate(
        [pair_tile(fields, partner, cell_weight) for partner in partner_list], 0
    )
    tile_sums = jnp.dot(products, resolution_basis, preferred_element_type=jnp.float32)
    tile_sums = tile_sums.reshape(reach_count, square, columns) * live_tiles[:, None, None].astype(
        jnp.float32
    )
    tile_table = tile_sums.reshape(reach_count * square, columns)
    tile_table = lax.psum_scatter(tile_table, "cell", scatter_dimension=1, tiled=True)
    owners_count = lax.axis_size("elec")
    candidates_here = quadrupoles.shape[0]
    capacity = 2 * ((candidates_here + owners_count - 1) // owners_count)
    owner_block = quadrupoles[:, 0] // electrodes
    offset_block = quadrupoles[:, 2] // electrodes - owner_block
    local_index = quadrupoles % electrodes
    chosen = (owner_block[:, None] == jnp.arange(owners_count)[None, :]).astype(jnp.int32)
    slot_index = jnp.sum(jnp.cumsum(chosen, 0) * chosen, 1) - 1
    tile_base = offset_block * square
    entries = jnp.stack(
        [
            tile_base + local_index[:, 0] * electrodes + local_index[:, 2],
            tile_base + local_index[:, 0] * electrodes + local_index[:, 3],
            tile_base + local_index[:, 1] * electrodes + local_index[:, 2],
            tile_base + local_index[:, 1] * electrodes + local_index[:, 3],
            jnp.ones_like(tile_base),
        ],
        1,
    )
    requests = (
        jnp.zeros((owners_count, capacity, 5), jnp.int32).at[owner_block, slot_index].set(entries)
    )
    received = lax.all_to_all(requests, "elec", split_axis=0, concat_axis=0, tiled=True)

    def pick_rows(column):
        return jnp.take(tile_table, received[:, :, column], axis=0)

    combined = pick_rows(0) - pick_rows(1) - pick_rows(2) + pick_rows(3)
    combined = combined * received[:, :, 4:5].astype(jnp.float32)
    returned = lax.all_to_all(combined, "elec", split_axis=0, concat_axis=0, tiled=True)
    own_rows = returned[owner_block, slot_index]
    scattered = own_rows.T
    energy = lax.psum(jnp.sum(scattered * scattered, axis=0), "cell")
    full_rank = resolution_basis.shape[1]
    return (scattered, jnp.log1p(energy / full_rank))


def solution(mesh):
    placed = (P("elec", None, "cell"), P("cell"), P("cell", None), P("elec", None), P("elec", None))
    return jax.shard_map(
        per_device,
        mesh=mesh,
        in_specs=placed,
        out_specs=(P("cell", "elec"), P("elec")),
        check_vma=False,
    )
```

profile of v0, /device:TPU:1, one launch (start us, length us, event | category | flops | bytes accessed | tf_op | source)
XLA Modules:
  0.0 223.4 jit_solution(2531084430299442341)
XLA Ops:
  7.2 0.0 reduce-scatter.2.cloned.1.call-start
  7.2 1.3 collective-permute-start
  8.5 1.3 collective-permute-start.1
  9.8 1.3 collective-permute-start.2
  11.1 1.2 convert_element_type.49
  12.4 0.1 slice_bitcast_fusion.11
  12.5 0.7 convert_bitcast_fusion.1
  13.1 0.1 broadcast_bitcast_fusion
  13.2 24.5 %collective-permute-done = bf16[16,3,8192]{2,0,1:T(8,128)(2,1)S(1)} collective-permute-done((bf16[16,3,8192]{2,0,1:T(8,128)(2,1)}, bf16[16,3,8192]{2,0,1:T(8,128)(2,1)S(1)}, u32[]{:S(2)}, u32[]{:S(2)}) %collective-permute-start) | collective-permute-done | bytes 786464 | tf_op jit(solution)/shard_map/ppermute | solution.py:10
  37.7 0.1 convert_element_type.51
  37.8 0.1 slice_bitcast_fusion.8
  37.9 10.0 %collective-permute-done.1 = bf16[16,3,8192]{2,0,1:T(8,128)(2,1)S(1)} collective-permute-done((bf16[16,3,8192]{2,0,1:T(8,128)(2,1)}, bf16[16,3,8192]{2,0,1:T(8,128)(2,1)S(1)}, u32[]{:S(2)}, u32[]{:S(2)}) %collective-permute-start.1) | collective-permute-done | bytes 786464 | tf_op jit(solution)/shard_map/ppermute | solution.py:10
  47.9 0.1 convert_element_type.53
  48.1 0.1 slice_bitcast_fusion.5
  48.2 0.0 collective-permute-done.2
  48.2 0.1 convert_element_type.55
  48.3 1.2 slice_bitcast_fusion.2
  49.4 13.3 %multiply_add_fusion.3 = (f32[16,16,8192]{2,1,0:T(8,128)}, f32[16,16,8192]{2,1,0:T(8,128)}, f32[16,16,8192]{2,1,0:T(8,128)}, f32[16,16,8192]{2,1,0:T(8,128)}) fusion(f32[16,8192]{1,0:T(8,128)S(1)} %get-tuple-element.29, f32[16,8192]{1,0:T(8,128)S(1)} %get-tuple-element.30, f32[16,8192]{1,0:T(8,128)S(1)} %get-tuple-element.28, ...), kind=kLoop, calls=%fused_computation.25 | loop fusion | flops 41943040 | bytes 39845888 | tf_op jit(solution)/shard_map/add | solution.py:18
  62.8 0.0 copy-done
  62.8 18.3 %fusion.11 = (bf16[256,8192]{1,0:T(8,128)(2,1)}, bf16[256,8192]{1,0:T(8,128)(2,1)}, bf16[256,8192]{1,0:T(8,128)(2,1)}, bf16[256,8192]{1,0:T(8,128)(2,1)}) fusion(f32[16,16,8192]{2,1,0:T(8,128)} %get-tuple-element.18, f32[8192]{0:T(1024)S(1)} %copy-done, f32[16,16,8192]{2,1,0:T(8,128)} %get-tuple-element.21, f32[16,16,8192]{2,1,0:T(8,128)} %get-tuple-element.19, ...), kind=kLoop, calls=%fused_computation.21 | loop fusion | flops 16777216 | bytes 50364416 | tf_op jit(solution)/shard_map/convert_element_type | solution.py:20
  81.1 14.7 %fusion.12 = f32[1024,512]{0,1:T(8,128)} fusion(bf16[8192,512]{1,0:T(8,128)(2,1)} %param.9, bf16[256,8192]{1,0:T(8,128)(2,1)} %get-tuple-element.42, bf16[256,8192]{1,0:T(8,128)(2,1)} %get-tuple-element.41, bf16[256,8192]{1,0:T(8,128)(2,1)} %get-tuple-element.40, bf16[256,8192]{1,0:T(8,128)(2,1)} %get-tuple-element.39, f32[1024]{0:T(1024)S(1)} %bitcast.96), kind=kOutput, calls=%fused_computation.26 | convolution fusion | flops 8657567744 | bytes 27267072 | tf_op jit(solution)/shard_map/dot_general | solution.py:35
  95.7 0.0 reduce-scatter.2.cloned.1.call-update
  95.8 0.1 fusion.16
  95.9 0.1 reduce_window_sum.11
  96.0 0.2 select_reduce_fusion
  96.2 0.1 copy.78
  96.3 3.6 %scatter_fusion = s32[32,4,5]{2,1,0:T(4,128)S(1)} fusion(s32[32,4,5]{2,1,0:T(4,128)S(1)} %broadcast_in_dim.8, s32[64]{0:T(128)S(1)} %get-tuple-element.16, s32[64,5]{1,0:T(8,128)S(1)} %copy.78), kind=kCustom, calls=%fused_computation.5 | custom fusion | bytes 4352 | tf_op jit(solution)/shard_map/scatter | solution.py:61
  99.9 60.9 %all_to_all.10 = s32[32,4,5]{2,1,0:T(4,128)S(1)} all-to-all(s32[32,4,5]{2,1,0:T(4,128)S(1)} %scatter_fusion), channel_id=1, replica_groups=mesh['elec'=32,'cell'=8] {'elec'}, dimensions={0} | all-to-all | bytes 5120 | tf_op jit(solution)/shard_map/all_to_all | solution.py:63
  160.8 0.2 fusion.22
  161.0 0.1 copy.79
  161.1 0.1 copy.81
  161.2 0.1 reshape.153
  161.3 0.1 copy.83
  161.4 0.1 copy.85
  161.5 0.1 reshape.157
  161.6 0.1 copy.87
  161.7 0.1 copy.89
  161.8 0.1 reshape.161
  161.9 0.1 copy.91
  162.1 0.1 copy.93
  162.1 0.1 reshape.165
  162.3 0.1 copy.80
  162.4 0.1 copy.84
  162.5 0.1 copy.88
  162.6 0.1 copy.92
  162.7 0.1 copy.98
  162.8 0.1 copy.96
  163.0 11.8 %reduce-scatter.2.cloned.1.call-done = f32[1024,64]{0,1:T(8,128)} async-done(((f32[1024,512]{0,1:T(8,128)}), f32[1024,64]{0,1:T(8,128)}) %reduce-scatter.2.cloned.1.call-update) | async-done | bytes 262160 | tf_op jit(solution)/shard_map/reduce_scatter | solution.py:40
  174.7 1.1 copy.82
  175.9 0.6 gather_fusion.1
  176.5 0.6 gather_fusion.2
  177.2 0.6 gather_fusion.3
  177.8 0.6 gather_fusion.4
  178.5 0.2 fusion.15
  178.7 0.1 reshape.169
  178.8 17.8 %all_to_all.11 = f32[32,1,256]{2,1,0:T(1,128)S(1)} all-to-all(f32[32,1,256]{2,1,0:T(1,128)S(1)} %reshape.169), channel_id=1, replica_groups=mesh['elec'=32,'cell'=8] {'elec'}, dimensions={0} | all-to-all | bytes 65536 | tf_op jit(solution)/shard_map/all_to_all | solution.py:70
  196.6 0.5 broadcast.268
  197.1 0.7 reduce
  197.8 0.1 reshape.170
  197.9 0.8 gather_fusion
  198.7 0.1 multiply_reduce_fusion
  198.8 0.7 copy.97
  199.6 16.5 %psum.7 = f32[64]{0:T(128)S(1)} all-reduce(f32[64]{0:T(128)S(1)} %multiply_reduce_fusion), channel_id=1, replica_groups=mesh['elec'=32,'cell'=8] {'cell'}, use_global_device_ids=true, to_apply=%region_5.7 | all-reduce | flops 64 | bytes 512 | tf_op jit(solution)/shard_map/psum | solution.py:73
  216.0 0.5 multiply_log-plus-one_fusion
  (23 shorter events, 0.2 us)
Async XLA Ops:
  7.2 167.6 %reduce-scatter.2.cloned.1.call-start = ((), (), s32[]{:S(2)}) async-start(), calls=%async_computation.3 | async-start | bytes 2359296 | tf_op jit(solution)/shard_map/reduce_scatter | solution.py:40
  7.2 30.5 %collective-permute-start = (bf16[16,3,8192]{2,0,1:T(8,128)(2,1)}, bf16[16,3,8192]{2,0,1:T(8,128)(2,1)S(1)}, u32[]{:S(2)}, u32[]{:S(2)}) collective-permute-start(bf16[16,3,8192]{2,0,1:T(8,128)(2,1)} %param.7), channel_id=1, source_target_pairs={{8,0},{16,8},{24,16},{32,24},{40,32},{48,40},{56,48},{64,56},{72,6... | collective-permute-start | bytes 2359304 | tf_op jit(solution)/shard_map/ppermute | solution.py:10
  8.5 39.4 %collective-permute-start.1 = (bf16[16,3,8192]{2,0,1:T(8,128)(2,1)}, bf16[16,3,8192]{2,0,1:T(8,128)(2,1)S(1)}, u32[]{:S(2)}, u32[]{:S(2)}) collective-permute-start(bf16[16,3,8192]{2,0,1:T(8,128)(2,1)} %param.7), channel_id=1, source_target_pairs={{16,0},{24,8},{32,16},{40,24},{48,32},{56,40},{64,48},{72,56},{80,... | collective-permute-start | bytes 2359304 | tf_op jit(solution)/shard_map/ppermute | solution.py:10
  9.8 38.4 %collective-permute-start.2 = (bf16[16,3,8192]{2,0,1:T(8,128)(2,1)}, bf16[16,3,8192]{2,0,1:T(8,128)(2,1)S(1)}, u32[]{:S(2)}, u32[]{:S(2)}) collective-permute-start(bf16[16,3,8192]{2,0,1:T(8,128)(2,1)} %param.7), channel_id=1, source_target_pairs={{24,0},{32,8},{40,16},{48,24},{56,32},{64,40},{72,48},{80,56},{88,... | collective-permute-start | bytes 2359304 | tf_op jit(solution)/shard_map/ppermute | solution.py:10
  49.4 13.3 %copy-start = (f32[8192]{0:T(1024)S(1)}, f32[8192]{0:T(1024)}, u32[]{:S(2)}) copy-start(f32[8192]{0:T(1024)} %param.8) | copy-start | bytes 98308
  81.1 14.7 %copy-start.1 = (s32[64,4]{0,1:T(4,128)S(1)}, s32[64,4]{0,1:T(4,128)}, u32[]{:S(2)}) copy-start(s32[64,4]{0,1:T(4,128)} %param.11) | copy-start | bytes 3076
Sparse Core Ops, SparseCore 0:
  95.9 78.8 reduce-scatter.1
where the time goes:
time: 224 us; the launch traced here: 223 us
  blocking collectives  95.2 us (42%)
  waiting for transfers between devices  46.3 us (21%)
  other arithmetic  35.9 us (16%)
  matrix products  14.7 us (7%)
  between operations  14.3 us (6%)
  local copies, waits for them, and re-layouts  13.2 us (6%)
  starting transfers between devices  3.91 us (2%)
    all_to_all x1, blocking collectives, per_device(): lax.all_to_all(requests, 'elec', split_axis=0, concat_axis=0, tiled=True)  60.9 us
    ppermute x3, waiting for transfers between devices, from_behind(): return lax.ppermute(block, axis, route)  34.5 us
    convert_element_type x1, other arithmetic, pair_tile(): return (summed * cell_weight).astype(jnp.bfloat16).reshape(number, -1)  18.3 us
    all_to_all x1, blocking collectives, per_device(): lax.all_to_all(combined, 'elec', split_axis=0, concat_axis=0, tiled=True)  17.8 us
    psum x1, blocking collectives, per_device(): energy = lax.psum(jnp.sum(scattered * scattered, axis=0), 'cell')  16.5 us
    dot_general x1, matrix products, per_device(): jnp.dot(products, resolution_basis, preferred_element_type=jnp.float32)  14.7 us
    add x1, other arithmetic, pair_tile(): summed = summed + left_wide[:, None, 2, :] * right_wide[None, :, 2, :]  13.3 us
    reduce_scatter x1, waiting for transfers between devices, per_device(): lax.psum_scatter(tile_table, 'cell', scatter_dimension=1, tiled=True)  11.8 us
  transfers between devices with their start and end apart: 4, of which 3 were waited for; matrix products, arithmetic and copies ran while one was open for 4% of the time, Pallas kernels for 0%

commit v1 on v0

v1 whole, which is shorter than its diff:
```python
import functools

import jax
import jax.numpy as jnp
from jax import lax
from jax.experimental import pallas as pl
from jax.experimental.pallas import tpu as pltpu
from jax.sharding import PartitionSpec as P

NY = 4
NX = 4
CORES = 2
CAP = 4
MESH = pl.DeviceIdType.MESH


def kernel(
    sizes,
    fields,
    weight,
    basis,
    pattern,
    quads,
    projection,
    energy,
    rows,
    basis_here,
    basis_turned,
    weight_here,
    asked,
    onehot,
    partial,
    from_core,
    core_sum,
    from_x,
    x_sum,
    from_y,
    to_z,
    from_z,
    own_energy,
    energies,
    local_sem,
    ask_send,
    ask_y,
    ask_z_send,
    ask_z,
    fy_send,
    fy_recv,
    fz_send,
    fz_recv,
    core_send,
    core_recv,
    x_send,
    x_recv,
    y_send,
    y_recv,
    z_send,
    z_recv,
    e_send,
    e_recv,
):
    nz, block, cells, chunks, slots, rank, here = sizes
    quarter = cells // NY
    width = quarter // chunks
    half = NY * nz * NY * slots
    elec = lax.axis_index("elec")
    cell = lax.axis_index("cell")
    z, y = lax.div(elec, NY), lax.rem(elec, NY)
    x, core = lax.div(cell, CORES), lax.rem(cell, CORES)

    def turn(value, step, size):
        return lax.rem(value + step, size)

    def at_y(other):
        return (z * NY + other, cell)

    def at_z(other):
        return (other * NY + y, cell)

    def at_cell(other):
        return (elec, other)

    def remote(src, dst, send, recv, device):
        return pltpu.make_async_remote_copy(
            src_ref=src, dst_ref=dst, send_sem=send, recv_sem=recv, device_id=device, device_id_type=MESH
        )

    load_basis = pltpu.make_async_copy(basis.at[pl.ds(y * quarter, quarter)], basis_here, local_sem.at[0])
    load_weight = pltpu.make_async_copy(weight.at[:, pl.ds(y * quarter, quarter)], weight_here, local_sem.at[1])
    load_own = pltpu.make_async_copy(
        fields.at[:, :, pl.ds(y * quarter, quarter)], rows.at[:, pl.ds(y * block, block), :], local_sem.at[2]
    )
    load_basis.start()
    load_weight.start()
    load_own.start()

    with jax.named_scope("barrier"):
        barrier = pltpu.get_barrier_semaphore()
        for d in range(1, NY):
            pl.semaphore_signal(barrier, inc=1, device_id=at_y(turn(y, d, NY)), device_id_type=MESH)
        for d in range(1, nz):
            pl.semaphore_signal(barrier, inc=1, device_id=at_z(turn(z, d, nz)), device_id_type=MESH)
        for d in range(1, NX * CORES):
            pl.semaphore_signal(barrier, inc=1, device_id=at_cell(turn(cell, d, NX * CORES)), device_id_type=MESH)
        pads = (NY * 2 - 1) * block
        rows[:, pads:, :] = jnp.zeros((3, rows.shape[1] - pads, quarter), jnp.bfloat16)
        asked[y, z] = jnp.full(asked.shape[2:], -1, jnp.int32)
        asked[y, z, 0:4, 0:here] = quads[...]
        asked[y, z, 4:5, 0 : pattern.shape[1]] = pattern[...]
        pl.semaphore_wait(barrier, NY - 1 + nz - 1 + NX * CORES - 1)

    ask_copies = []
    for d in range(1, NY):
        ask_copies.append(
            remote(asked.at[y, z], asked.at[y, z], ask_send.at[d], ask_y.at[d], at_y(turn(y, d, NY)))
        )
        ask_copies[-1].start()

    def y_copy(c, d):
        target = turn(y, d, NY)
        return remote(
            fields.at[:, :, pl.ds(target * quarter + c * width, width)],
            rows.at[:, pl.ds(y * block, block), pl.ds(c * width, width)],
            fy_send.at[c, d],
            fy_recv.at[c, d],
            at_y(target),
        )

    above = at_z(turn(z, nz - 1, nz))

    def z_own(c):
        return remote(
            fields.at[:, :, pl.ds(y * quarter + c * width, width)],
            rows.at[:, pl.ds((NY + y) * block, block), pl.ds(c * width, width)],
            fz_send.at[c, y],
            fz_recv.at[c, y],
            above,
        )

    def z_pass(c, b):
        return remote(
            rows.at[:, pl.ds(b * block, block), pl.ds(c * width, width)],
            rows.at[:, pl.ds((NY + b) * block, block), pl.ds(c * width, width)],
            fz_send.at[c, b],
            fz_recv.at[c, b],
            above,
        )

    for c in range(chunks):
        for d in (2, 1, 3):
            y_copy(c, d).start()

        @pl.when(y < NY - 1)
        def _(c=c):
            z_own(c).start()

    with jax.named_scope("ask"):
        for d in range(1, NY):
            ask_copies[d - 1].wait_recv()
        for d in range(1, nz):
            ask_copies.append(
                remote(asked.at[:, z], asked.at[:, z], ask_z_send.at[d], ask_z.at[d], at_z(turn(z, d, nz)))
            )
            ask_copies[-1].start()

    with jax.named_scope("turn_basis"):
        load_basis.wait()
        basis_turned[...] = basis_here[...].T
        load_weight.wait()
        load_own.wait()

    def forward(c):
        with jax.named_scope("forward"):
            for d in (1, 3, 2):
                y_copy(c, d).wait_recv()
                source = turn(y, NY - d, NY)

                @pl.when(source < NY - 1)
                def _(c=c, source=source):
                    z_pass(c, source).start()

    forward(0)

    lanes = asked.shape[-1]
    earlier = (
        lax.broadcasted_iota(jnp.int32, (lanes, lanes), 0) < lax.broadcasted_iota(jnp.int32, (lanes, lanes), 1)
    ).astype(jnp.bfloat16)

    def slot_match(in_block, slot):
        before = jnp.dot(in_block.astype(jnp.bfloat16), earlier, preferred_element_type=jnp.float32)
        return jnp.logical_and(in_block > 0.5, before == slot.astype(jnp.float32))

    with jax.named_scope("onehot"):
        for d in range(1, nz):
            ask_copies[NY - 1 + d - 1].wait_recv()
        devices = NY * nz
        group = NY * slots

        def wide(row):
            line = asked[:, :, row, :].reshape(devices, 1, lanes)
            return jnp.broadcast_to(line, (devices, group, lanes))

        inner = lax.broadcasted_iota(jnp.int32, (devices, group, lanes), 1)
        a_wide = wide(0)
        in_block = jnp.where(lax.shift_right_arithmetic(a_wide, 4) == z * NY + lax.div(inner, slots), 1.0, 0.0)
        in_block = in_block.reshape(half, lanes)
        slot = lax.rem(inner, slots).reshape(half, lanes)
        match = slot_match(in_block, slot)
        lane = lax.broadcasted_iota(jnp.int32, (half, lanes), 1)

        def local(row):
            value = (wide(row) - (z * NY * block - 1)).reshape(half, lanes).astype(jnp.float32)
            return jnp.sum(jnp.where(match, value, 0.0), axis=1, keepdims=True)

        a, b, m, n = (local(row).astype(jnp.int32) for row in range(4))
        offset = lax.shift_right_arithmetic(m - 1, 4) - lax.shift_right_arithmetic(a - 1, 4)
        used = asked[:, z, 4, :].reshape(NY, 1, lanes)
        used = jnp.broadcast_to(used, (NY, slots, lanes)).reshape(1, group, lanes)
        used = jnp.broadcast_to(used, (devices, group, lanes)).reshape(half, lanes)
        live = jnp.sum(jnp.where(lane == offset, used.astype(jnp.float32), 0.0), axis=1, keepdims=True)
        one = jnp.where(lane == a - 1, 1.0, 0.0) - jnp.where(lane == b - 1, 1.0, 0.0)
        onehot[0:half] = (live * one).astype(jnp.bfloat16)
        two = jnp.where(lane == m - 1, 1.0, 0.0) - jnp.where(lane == n - 1, 1.0, 0.0)
        onehot[half : 2 * half] = two.astype(jnp.bfloat16)

    def compute(c):
        with jax.named_scope("gather_fields"):
            for b in range(NY - 1):
                z_pass(c, b).wait_recv()
        with jax.named_scope("sensitivity"):
            span = slice(c * width, (c + 1) * width)
            total = None
            for component in range(3):
                picked = jnp.dot(onehot[...], rows[component, :, span], preferred_element_type=jnp.float32)
                term = picked[:half] * picked[half:]
                total = term if total is None else total + term
            sensitivity = (total * weight_here[:, span]).astype(jnp.bfloat16)
            part = lax.dot_general(
                basis_turned[:, span],
                sensitivity,
                (((1,), (1,)), ((), ())),
                preferred_element_type=jnp.float32,
            ).reshape(partial.shape)
            partial[...] = part if c == 0 else partial[...] + part

    for c in range(chunks):
        if c + 1 < chunks:
            forward(c + 1)
        compute(c)

    with jax.named_scope("sum_core"):
        sibling = at_cell(x * CORES + (1 - core))
        for d in (2, 1, 3, 0):
            target = turn(x, d, NX)
            remote(
                partial.at[target, 1 - core], from_core.at[target], core_send.at[d], core_recv.at[d], sibling
            ).start()

    def core_copy(d):
        target = turn(x, d, NX)
        return remote(
            partial.at[target, 1 - core], from_core.at[target], core_send.at[d], core_recv.at[d], sibling
        )

    def x_copy(d):
        target = turn(x, d, NX)
        return remote(
            core_sum.at[target], from_x.at[d], x_send.at[d], x_recv.at[d], at_cell(target * CORES + core)
        )

    with jax.named_scope("sum_x"):
        for d in (2, 1, 3, 0):
            target = turn(x, d, NX)
            core_copy(d).wait_recv()
            core_sum[target] = partial[target, core] + from_core[target]
            if d:
                x_copy(d).start()
        total = core_sum[x]
        for d in (1, 3, 2):
            x_copy(d).wait_recv()
            total = total + from_x[d]

    lane_group = nz * NY * slots
    with jax.named_scope("sum_y"):
        for other in range(NY):
            x_sum[other] = total[:, other * lane_group : (other + 1) * lane_group]

        def y_sum_copy(d):
            target = turn(y, d, NY)
            return remote(x_sum.at[target], from_y.at[d], y_send.at[d], y_recv.at[d], at_y(target))

        for d in (2, 1, 3):
            y_sum_copy(d).start()
        total = x_sum[y]
        for d in (1, 3, 2):
            y_sum_copy(d).wait_recv()
            total = total + from_y[d]

    with jax.named_scope("return_z"):
        part = total.shape[0]
        spread = jnp.concatenate([total, jnp.zeros((lanes - part, lane_group), jnp.float32)], axis=0)
        to_z[...] = spread.T.reshape(to_z.shape)

        def z_copy(d):
            target = turn(z, d, nz)
            return remote(to_z.at[target], from_z.at[z], z_send.at[d], z_recv.at[d], at_z(target))

        for d in range(1, nz):
            z_copy(d).start()
        from_z[z] = to_z[z]
        slot_row = lax.broadcasted_iota(jnp.int32, (lane_group, lanes), 0)
        mine = jnp.broadcast_to(lax.shift_right_arithmetic(asked[y, z, 0:1, :], 4), (lane_group, lanes))
        own_block = jnp.where(mine == lax.div(slot_row, slots), 1.0, 0.0)
        own_match = slot_match(own_block, lax.rem(slot_row, slots)).astype(jnp.float32)
        for d in range(1, nz):
            z_copy(d).wait_recv()
        returned = from_z[...].reshape(lane_group, lanes).T
        own = jnp.dot(
            returned, own_match, precision=lax.Precision.HIGHEST, preferred_element_type=jnp.float32
        )
        projection[...] = own[:part, :here]

    with jax.named_scope("energies"):
        own_energy[...] = jnp.broadcast_to(jnp.sum(own * own, axis=0, keepdims=True), own_energy.shape)

        def e_copy(d):
            target = turn(cell, d, NX * CORES)
            return remote(own_energy, energies.at[d], e_send.at[d], e_recv.at[d], at_cell(target))

        for d in range(1, NX * CORES):
            e_copy(d).start()
        total = own_energy[...]
        for d in range(1, NX * CORES):
            e_copy(d).wait_recv()
            total = total + energies[d]
        energy[...] = total[0:1, :here]

    with jax.named_scope("drain"):
        for copy in ask_copies:
            copy.wait_send()
        for c in range(chunks):
            for d in range(1, NY):
                y_copy(c, d).wait_send()
            for b in range(NY - 1):
                z_pass(c, b).wait_send()
        for d in range(NX):
            core_copy(d).wait_send()
        for d in range(1, NX):
            x_copy(d).wait_send()
        for d in range(1, NY):
            y_sum_copy(d).wait_send()
        for d in range(1, nz):
            z_copy(d).wait_send()
        for d in range(1, NX * CORES):
            e_copy(d).wait_send()


def per_device(fields, cell_weight, resolution_basis, pattern, quadrupoles, chunks=4):
    block, components, cells = fields.shape
    rank = resolution_basis.shape[1]
    here = quadrupoles.shape[0]
    nz = lax.axis_size("elec") // NY
    quarter = cells // NY
    part = rank // (NX * CORES)
    lanes = 128
    slots = CAP
    half = nz * NY * NY * slots
    group = nz * NY * slots
    held = 2 * NY * block
    dma = pltpu.SemaphoreType.DMA
    vmem = pl.BlockSpec(memory_space=pltpu.VMEM)
    anywhere = pl.BlockSpec(memory_space=pl.ANY)
    sizes = (nz, block, cells, chunks, slots, rank, here)
    projection, energy = pl.pallas_call(
        functools.partial(kernel, sizes),
        out_shape=(
            jax.ShapeDtypeStruct((part, here), jnp.float32),
            jax.ShapeDtypeStruct((1, here), jnp.float32),
        ),
        in_specs=[anywhere, anywhere, anywhere, vmem, vmem],
        out_specs=(vmem, vmem),
        scratch_shapes=[
            pltpu.VMEM((components, held, quarter), jnp.bfloat16),
            pltpu.VMEM((quarter, rank), jnp.bfloat16),
            pltpu.VMEM((rank, quarter), jnp.bfloat16),
            pltpu.VMEM((1, quarter), jnp.float32),
            pltpu.VMEM((NY, nz, 8, lanes), jnp.int32),
            pltpu.VMEM((2 * half, lanes), jnp.bfloat16),
            pltpu.VMEM((NX, CORES, part, half), jnp.float32),
            pltpu.VMEM((NX, part, half), jnp.float32),
            pltpu.VMEM((NX, part, half), jnp.float32),
            pltpu.VMEM((NX, part, half), jnp.float32),
            pltpu.VMEM((NY, part, group), jnp.float32),
            pltpu.VMEM((NY, part, group), jnp.float32),
            pltpu.VMEM((nz, NY * slots, lanes), jnp.float32),
            pltpu.VMEM((nz, NY * slots, lanes), jnp.float32),
            pltpu.VMEM((8, lanes), jnp.float32),
            pltpu.VMEM((NX * CORES, 8, lanes), jnp.float32),
            dma((3,)),
            dma((NY,)),
            dma((NY,)),
            dma((nz,)),
            dma((nz,)),
            dma((chunks, NY)),
            dma((chunks, NY)),
            dma((chunks, NY)),
            dma((chunks, NY)),
            dma((NX,)),
            dma((NX,)),
            dma((NX,)),
            dma((NX,)),
            dma((NY,)),
            dma((NY,)),
            dma((nz,)),
            dma((nz,)),
            dma((NX * CORES,)),
            dma((NX * CORES,)),
        ],
        compiler_params=pltpu.CompilerParams(
            collective_id=0, has_side_effects=True, vmem_limit_bytes=48 * 1024 * 1024
        ),
    )(
        fields.transpose(1, 0, 2),
        cell_weight.reshape(1, cells),
        resolution_basis,
        pattern,
        quadrupoles.T,
    )
    return projection, jnp.log1p(energy.reshape(here) / rank)


def solution(mesh):
    placed = (P("elec", None, "cell"), P("cell"), P("cell", None), P("elec", None), P("elec", None))
    return jax.shard_map(
        per_device,
        mesh=mesh,
        in_specs=placed,
        out_specs=(P("cell", "elec"), P("elec")),
        check_vma=False,
    )
```

time: 224 us -> 59.5 us (0.27)
  blocking collectives: 95.2 us -> 0 us
  Pallas kernels: 0 us -> 54.3 us
  waiting for transfers between devices: 46.3 us -> 0 us
  other arithmetic: 35.9 us -> 0.52 us
  matrix products: 14.7 us -> 0 us
  between operations: 14.3 us -> 0.65 us
  local copies, waits for them, and re-layouts: 13.2 us -> 3.83 us
  starting transfers between devices: 3.91 us -> 0 us
    all_to_all x2 -> x0, blocking collectives: 78.7 us -> none  [the longest x1 60.9 us: per_device(): lax.all_to_all(requests, 'elec', split_axis=0, concat_axis=0, tiled=True)]
    pallas_call x0 -> x1, Pallas kernels: none -> 54.3 us  [per_device(): pl.pallas_call(functools.partial(kernel, sizes), out_shape=(jax.ShapeDtyp...]
    ppermute x3 -> x0, waiting for transfers between devices: 34.5 us -> none  [from_behind(): return lax.ppermute(block, axis, route)]
    convert_element_type x7 -> x0, other arithmetic: 20.6 us -> none  [the longest x1 18.3 us: pair_tile(): return (summed * cell_weight).astype(jnp.bfloat16).reshape(number, -1)]
    psum x1 -> x0, blocking collectives: 16.5 us -> none  [per_device(): energy = lax.psum(jnp.sum(scattered * scattered, axis=0), 'cell')]
    dot_general x1 -> x0, matrix products: 14.7 us -> none  [per_device(): jnp.dot(products, resolution_basis, preferred_element_type=jnp.float32)]
    add x2 -> x0, other arithmetic: 13.3 us -> none  [the longest x1 13.3 us: pair_tile(): summed = summed + left_wide[:, None, 2, :] * right_wide[None, :, 2, :]]
    reduce_scatter x1 -> x0, waiting for transfers between devices: 11.8 us -> none  [per_device(): lax.psum_scatter(tile_table, 'cell', scatter_dimension=1, tiled=True)]
  transfers between devices with their start and end apart: 4 -> 0, of which waited for: 3 -> 0; matrix products, arithmetic and copies ran while one was open for 4% -> 0% of each run, Pallas kernels for 0% -> 0%
where the time goes in v1:
time: 59.5 us; the launch traced here: 59.3 us
  Pallas kernels  54.3 us (91%)
  local copies, waits for them, and re-layouts  3.83 us (6%)
  between operations  0.65 us (1%)
    pallas_call x1, Pallas kernels, per_device(): pl.pallas_call(functools.partial(kernel, sizes), out_shape=(jax.ShapeDtyp...  54.3 us
    unnamed x9, local copies, waits for them, and re-layouts  3.83 us

profile of v1, /device:TPU:1, one launch (start us, length us, event | category | flops | bytes accessed | tf_op | source)
XLA Modules:
  0.0 59.3 jit_solution(17429034242538946683)
XLA Ops:
  0.6 0.0 copy-start
  0.6 1.1 %copy-done = bf16[16,3,8192]{2,0,1:T(8,128)(2,1)S(1)} copy-done((bf16[16,3,8192]{2,0,1:T(8,128)(2,1)S(1)}, bf16[16,3,8192]{2,0,1:T(8,128)(2,1)}, u32[]{:S(2)}) %copy-start) | copy-done | bytes 786456
  1.8 0.0 copy-start.1
  1.8 0.8 %copy-done.1 = f32[8192]{0:T(1024)S(1)} copy-done((f32[8192]{0:T(1024)S(1)}, f32[8192]{0:T(1024)}, u32[]{:S(2)}) %copy-start.1) | copy-done | bytes 32792
  2.5 0.0 copy-start.2
  2.5 0.7 %copy-done.2 = s32[64,4]{0,1:T(4,128)S(1)} copy-done((s32[64,4]{0,1:T(4,128)S(1)}, s32[64,4]{0,1:T(4,128)}, u32[]{:S(2)}) %copy-start.2) | copy-done | bytes 1048
  3.2 0.0 copy-start.3
  3.2 0.7 %copy-done.3 = s32[1,4]{1,0:T(1,128)S(1)} copy-done((s32[1,4]{1,0:T(1,128)S(1)}, s32[1,4]{1,0:T(1,128)}, u32[]{:S(2)}) %copy-start.3) | copy-done | bytes 40
  3.9 54.3 %shard_map.68 = (f32[64,64]{1,0:T(8,128)S(1)}, f32[1,64]{1,0:T(1,128)S(1)}) custom-call(bf16[3,16,8192]{2,1,0:T(8,128)(2,1)S(1)} %bitcast.5, f32[1,8192]{1,0:T(1,128)S(1)} %bitcast.6, bf16[8192,512]{1,0:T(8,128)(2,1)} %basis.1, s32[1,4]{1,0:T(1,128)S(1)} %copy-done.3, s32[4,64]{1,0:T(4,128)S(1)} %bitcast.7), custom_call_target="tpu_custom_call" | custom-call | tf_op jit(solution)/shard_map/pallas_call | solution.py:374
  58.2 0.5 log-plus-one_bitcast_fusion
  58.7 0.6 %copy.8 = f32[64,64]{1,0:T(8,128)} copy(f32[64,64]{1,0:T(8,128)S(1)} %get-tuple-element.8) | data formatting | bytes 32768
Async XLA Ops:
  0.6 1.1 %copy-start = (bf16[16,3,8192]{2,0,1:T(8,128)(2,1)S(1)}, bf16[16,3,8192]{2,0,1:T(8,128)(2,1)}, u32[]{:S(2)}) copy-start(bf16[16,3,8192]{2,0,1:T(8,128)(2,1)} %param.5) | copy-start | bytes 2359300
  1.8 0.8 %copy-start.1 = (f32[8192]{0:T(1024)S(1)}, f32[8192]{0:T(1024)}, u32[]{:S(2)}) copy-start(f32[8192]{0:T(1024)} %param.6) | copy-start | bytes 98308
  2.5 0.7 %copy-start.2 = (s32[64,4]{0,1:T(4,128)S(1)}, s32[64,4]{0,1:T(4,128)}, u32[]{:S(2)}) copy-start(s32[64,4]{0,1:T(4,128)} %param.9) | copy-start | bytes 3076
  3.2 0.7 %copy-start.3 = (s32[1,4]{1,0:T(1,128)S(1)}, s32[1,4]{1,0:T(1,128)}, u32[]{:S(2)}) copy-start(s32[1,4]{1,0:T(1,128)} %pattern.1) | copy-start | bytes 52

commit v2 on v1

--- a/solution.py
+++ b/solution.py
@@ -25,20 +25,25 @@
     energy,
     rows,
     basis_here,
-    basis_turned,
     weight_here,
     asked,
     onehot,
+    pick,
     partial,
     from_core,
-    core_sum,
-    from_x,
-    x_sum,
+    own_sum,
+    to_y,
     from_y,
     to_z,
     from_z,
+    mine,
+    from_x,
+    turned,
+    from_sibling,
     own_energy,
-    energies,
+    sibling_energy,
+    pattern_here,
+    quads_here,
     local_sem,
     ask_send,
     ask_y,
@@ -56,13 +61,14 @@
     y_recv,
     z_send,
     z_recv,
-    e_send,
-    e_recv,
+    last_send,
+    last_recv,
 ):
     nz, block, cells, chunks, slots, rank, here = sizes
     quarter = cells // NY
     width = quarter // chunks
-    half = NY * nz * NY * slots
+    lane_group = nz * NY * slots
+    half = NY * lane_group
     elec = lax.axis_index("elec")
     cell = lax.axis_index("cell")
     z, y = lax.div(elec, NY), lax.rem(elec, NY)
@@ -79,6 +85,8 @@
 
     def at_cell(other):
         return (elec, other)
+
+    sibling = at_cell(x * CORES + (1 - core))
 
     def remote(src, dst, send, recv, device):
         return pltpu.make_async_remote_copy(
@@ -90,24 +98,32 @@
     load_own = pltpu.make_async_copy(
         fields.at[:, :, pl.ds(y * quarter, quarter)], rows.at[:, pl.ds(y * block, block), :], local_sem.at[2]
     )
+    load_quads = pltpu.make_async_copy(quads, quads_here, local_sem.at[3])
+    load_pattern = pltpu.make_async_copy(pattern, pattern_here, local_sem.at[4])
+    load_quads.start()
+    load_pattern.start()
     load_basis.start()
     load_weight.start()
     load_own.start()
 
     with jax.named_scope("barrier"):
         barrier = pltpu.get_barrier_semaphore()
+        for d in range(1, nz):
+            pl.semaphore_signal(barrier, inc=1, device_id=at_z(turn(z, d, nz)), device_id_type=MESH)
         for d in range(1, NY):
             pl.semaphore_signal(barrier, inc=1, device_id=at_y(turn(y, d, NY)), device_id_type=MESH)
-        for d in range(1, nz):
-            pl.semaphore_signal(barrier, inc=1, device_id=at_z(turn(z, d, nz)), device_id_type=MESH)
-        for d in range(1, NX * CORES):
-            pl.semaphore_signal(barrier, inc=1, device_id=at_cell(turn(cell, d, NX * CORES)), device_id_type=MESH)
+        for d in range(1, NX):
+            other = at_cell(turn(x, d, NX) * CORES + core)
+            pl.semaphore_signal(barrier, inc=1, device_id=other, device_id_type=MESH)
+        pl.semaphore_signal(barrier, inc=1, device_id=sibling, device_id_type=MESH)
         pads = (NY * 2 - 1) * block
         rows[:, pads:, :] = jnp.zeros((3, rows.shape[1] - pads, quarter), jnp.bfloat16)
         asked[y, z] = jnp.full(asked.shape[2:], -1, jnp.int32)
-        asked[y, z, 0:4, 0:here] = quads[...]
-        asked[y, z, 4:5, 0 : pattern.shape[1]] = pattern[...]
-        pl.semaphore_wait(barrier, NY - 1 + nz - 1 + NX * CORES - 1)
+        load_quads.wait()
+        load_pattern.wait()
+        asked[y, z, 0:4, 0:here] = quads_here[...]
+        asked[y, z, 4:5, 0 : pattern.shape[1]] = pattern_here[...]
+        pl.semaphore_wait(barrier, NY - 1 + nz - 1 + NX - 1 + CORES - 1)
 
     ask_copies = []
     for d in range(1, NY):
@@ -163,12 +179,6 @@
             )
             ask_copies[-1].start()
 
-    with jax.named_scope("turn_basis"):
-        load_basis.wait()
-        basis_turned[...] = basis_here[...].T
-        load_weight.wait()
-        load_own.wait()
-
     def forward(c):
         with jax.named_scope("forward"):
             for d in (1, 3, 2):
@@ -179,6 +189,7 @@
                 def _(c=c, source=source):
                     z_pass(c, source).start()
 
+    load_own.wait()
     forward(0)
 
     lanes = asked.shape[-1]
@@ -222,6 +233,14 @@
         onehot[0:half] = (live * one).astype(jnp.bfloat16)
         two = jnp.where(lane == m - 1, 1.0, 0.0) - jnp.where(lane == n - 1, 1.0, 0.0)
         onehot[half : 2 * half] = two.astype(jnp.bfloat16)
+
+        slot_row = lax.broadcasted_iota(jnp.int32, (lane_group, lanes), 0)
+        own_a = jnp.broadcast_to(lax.shift_right_arithmetic(asked[y, z, 0:1, :], 4), (lane_group, lanes))
+        own_block = jnp.where(own_a == lax.div(slot_row, slots), 1.0, 0.0)
+        own_match = slot_match(own_block, lax.rem(slot_row, slots)).astype(jnp.float32)
+        pick[...] = own_match.T[:here].astype(jnp.bfloat16)
+        load_basis.wait()
+        load_weight.wait()
 
     def compute(c):
         with jax.named_scope("gather_fields"):
@@ -234,13 +253,12 @@
                 picked = jnp.dot(onehot[...], rows[component, :, span], preferred_element_type=jnp.float32)
                 term = picked[:half] * picked[half:]
                 total = term if total is None else total + term
-            sensitivity = (total * weight_here[:, span]).astype(jnp.bfloat16)
-            part = lax.dot_general(
-                basis_turned[:, span],
-                sensitivity,
-                (((1,), (1,)), ((), ())),
-                preferred_element_type=jnp.float32,
-            ).reshape(partial.shape)
+            sensitivity = total * weight_here[:, span]
+            high = sensitivity.astype(jnp.bfloat16)
+            low = (sensitivity - high.astype(jnp.float32)).astype(jnp.bfloat16)
+            part = jnp.dot(high, basis_here[span, :], preferred_element_type=jnp.float32)
+            part = part + jnp.dot(low, basis_here[span, :], preferred_element_type=jnp.float32)
+            part = part.reshape(partial.shape)
             partial[...] = part if c == 0 else partial[...] + part
 
     for c in range(chunks):
@@ -248,92 +266,94 @@
             forward(c + 1)
         compute(c)
 
+    def own_half(other):
+        return pl.ds(pl.multiple_of(other * (rank // CORES), 128), rank // CORES)
+
+    def core_copy(d):
+        target = turn(y, d, NY)
+        return remote(
+            partial.at[target, :, own_half(1 - core)],
+            from_core.at[target],
+            core_send.at[d],
+            core_recv.at[d],
+            sibling,
+        )
+
+    def y_sum_copy(d):
+        target = turn(y, d, NY)
+        return remote(to_y.at[target], from_y.at[d], y_send.at[d], y_recv.at[d], at_y(target))
+
     with jax.named_scope("sum_core"):
-        sibling = at_cell(x * CORES + (1 - core))
         for d in (2, 1, 3, 0):
-            target = turn(x, d, NX)
-            remote(
-                partial.at[target, 1 - core], from_core.at[target], core_send.at[d], core_recv.at[d], sibling
-            ).start()
-
-    def core_copy(d):
-        target = turn(x, d, NX)
-        return remote(
-            partial.at[target, 1 - core], from_core.at[target], core_send.at[d], core_recv.at[d], sibling
-        )
+            core_copy(d).start()
+        for d in (2, 1, 3, 0):
+            target = turn(y, d, NY)
+            core_copy(d).wait_recv()
+            summed = partial[target, :, own_half(core)] + from_core[target]
+            if d:
+                to_y[target] = summed.astype(jnp.bfloat16)
+                y_sum_copy(d).start()
+            else:
+                own_sum[...] = summed
+
+    with jax.named_scope("sum_y"):
+        total = own_sum[...]
+        for d in (1, 3, 2):
+            y_sum_copy(d).wait_recv()
+            total = total + from_y[d].astype(jnp.float32)
+
+    def z_copy(d):
+        target = turn(z, d, nz)
+        return remote(to_z.at[target], from_z.at[z], z_send.at[d], z_recv.at[d], at_z(target))
+
+    with jax.named_scope("return_z"):
+        to_z[...] = total.astype(jnp.bfloat16).reshape(to_z.shape)
+        for d in (4, 3, 5, 2, 6, 1, 7):
+            if d < nz:
+                z_copy(d).start()
+        from_z[z] = to_z[z]
+        for d in range(1, nz):
+            z_copy(d).wait_recv()
+        returned = from_z[...].reshape(lane_group, rank // CORES)
+        mine[...] = jnp.dot(pick[...], returned, preferred_element_type=jnp.float32).astype(jnp.bfloat16)
 
     def x_copy(d):
         target = turn(x, d, NX)
-        return remote(
-            core_sum.at[target], from_x.at[d], x_send.at[d], x_recv.at[d], at_cell(target * CORES + core)
-        )
+        return remote(mine, from_x.at[d], x_send.at[d], x_recv.at[d], at_cell(target * CORES + core))
 
     with jax.named_scope("sum_x"):
-        for d in (2, 1, 3, 0):
-            target = turn(x, d, NX)
-            core_copy(d).wait_recv()
-            core_sum[target] = partial[target, core] + from_core[target]
-            if d:
-                x_copy(d).start()
-        total = core_sum[x]
+        for d in (2, 1, 3):
+            x_copy(d).start()
+        total = mine[...].astype(jnp.float32)
         for d in (1, 3, 2):
             x_copy(d).wait_recv()
-            total = total + from_x[d]
-
-    lane_group = nz * NY * slots
-    with jax.named_scope("sum_y"):
-        for other in range(NY):
-            x_sum[other] = total[:, other * lane_group : (other + 1) * lane_group]
-
-        def y_sum_copy(d):
-            target = turn(y, d, NY)
-            return remote(x_sum.at[target], from_y.at[d], y_send.at[d], y_recv.at[d], at_y(target))
-
-        for d in (2, 1, 3):
-            y_sum_copy(d).start()
-        total = x_sum[y]
-        for d in (1, 3, 2):
-            y_sum_copy(d).wait_recv()
-            total = total + from_y[d]
-
-    with jax.named_scope("return_z"):
-        part = total.shape[0]
-        spread = jnp.concatenate([total, jnp.zeros((lanes - part, lane_group), jnp.float32)], axis=0)
-        to_z[...] = spread.T.reshape(to_z.shape)
-
-        def z_copy(d):
-            target = turn(z, d, nz)
-            return remote(to_z.at[target], from_z.at[z], z_send.at[d], z_recv.at[d], at_z(target))
-
-        for d in range(1, nz):
-            z_copy(d).start()
-        from_z[z] = to_z[z]
-        slot_row = lax.broadcasted_iota(jnp.int32, (lane_group, lanes), 0)
-        mine = jnp.broadcast_to(lax.shift_right_arithmetic(asked[y, z, 0:1, :], 4), (lane_group, lanes))
-        own_block = jnp.where(mine == lax.div(slot_row, slots), 1.0, 0.0)
-        own_match = slot_match(own_block, lax.rem(slot_row, slots)).astype(jnp.float32)
-        for d in range(1, nz):
-            z_copy(d).wait_recv()
-        returned = from_z[...].reshape(lane_group, lanes).T
-        own = jnp.dot(
-            returned, own_match, precision=lax.Precision.HIGHEST, preferred_element_type=jnp.float32
-        )
-        projection[...] = own[:part, :here]
-
-    with jax.named_scope("energies"):
-        own_energy[...] = jnp.broadcast_to(jnp.sum(own * own, axis=0, keepdims=True), own_energy.shape)
-
-        def e_copy(d):
-            target = turn(cell, d, NX * CORES)
-            return remote(own_energy, energies.at[d], e_send.at[d], e_recv.at[d], at_cell(target))
-
-        for d in range(1, NX * CORES):
-            e_copy(d).start()
-        total = own_energy[...]
-        for d in range(1, NX * CORES):
-            e_copy(d).wait_recv()
-            total = total + energies[d]
-        energy[...] = total[0:1, :here]
+            total = total + from_x[d].astype(jnp.float32)
+        total = jnp.concatenate([total, jnp.zeros((lanes - here, rank // CORES), jnp.float32)], axis=0).T
+        turned[...] = total
+        own_energy[...] = jnp.broadcast_to(jnp.sum(total * total, axis=0, keepdims=True), own_energy.shape)
+
+    part = rank // (NX * CORES)
+    chip_rows = lax.rem(x * CORES * part, rank // CORES)
+    last = [
+        remote(
+            turned.at[pl.ds(pl.multiple_of(chip_rows + (1 - core) * part, 8), part)],
+            from_sibling,
+            last_send.at[0],
+            last_recv.at[0],
+            sibling,
+        ),
+        remote(own_energy, sibling_energy, last_send.at[1], last_recv.at[1], sibling),
+    ]
+    with jax.named_scope("cores"):
+        for copy in last:
+            copy.start()
+        for copy in last:
+            copy.wait_recv()
+        kept = turned[pl.ds(pl.multiple_of(chip_rows + core * part, 8), part)]
+        holder = lax.div(x * CORES * part, rank // CORES)
+        chosen = jnp.where(holder == core, kept, from_sibling[...])
+        projection[...] = chosen[:, :here]
+        energy[...] = (own_energy[...] + sibling_energy[...])[0:1, :here]
 
     with jax.named_scope("drain"):
         for copy in ask_copies:
@@ -343,16 +363,16 @@
                 y_copy(c, d).wait_send()
             for b in range(NY - 1):
                 z_pass(c, b).wait_send()
-        for d in range(NX):
+        for d in range(NY):
             core_copy(d).wait_send()
-        for d in range(1, NX):
-            x_copy(d).wait_send()
         for d in range(1, NY):
             y_sum_copy(d).wait_send()
         for d in range(1, nz):
             z_copy(d).wait_send()
-        for d in range(1, NX * CORES):
-            e_copy(d).wait_send()
+        for d in range(1, NX):
+            x_copy(d).wait_send()
+        for copy in last:
+            copy.wait_send()
 
 
 def per_device(fields, cell_weight, resolution_basis, pattern, quadrupoles, chunks=4):
@@ -377,26 +397,31 @@
             jax.ShapeDtypeStruct((part, here), jnp.float32),
             jax.ShapeDtypeStruct((1, here), jnp.float32),
         ),
-        in_specs=[anywhere, anywhere, anywhere, vmem, vmem],
+        in_specs=[anywhere] * 5,
         out_specs=(vmem, vmem),
         scratch_shapes=[
             pltpu.VMEM((components, held, quarter), jnp.bfloat16),
             pltpu.VMEM((quarter, rank), jnp.bfloat16),
-            pltpu.VMEM((rank, quarter), jnp.bfloat16),
             pltpu.VMEM((1, quarter), jnp.float32),
             pltpu.VMEM((NY, nz, 8, lanes), jnp.int32),
             pltpu.VMEM((2 * half, lanes), jnp.bfloat16),
-            pltpu.VMEM((NX, CORES, part, half), jnp.float32),
-            pltpu.VMEM((NX, part, half), jnp.float32),
-            pltpu.VMEM((NX, part, half), jnp.float32),
-            pltpu.VMEM((NX, part, half), jnp.float32),
-            pltpu.VMEM((NY, part, group), jnp.float32),
-            pltpu.VMEM((NY, part, group), jnp.float32),
-            pltpu.VMEM((nz, NY * slots, lanes), jnp.float32),
-            pltpu.VMEM((nz, NY * slots, lanes), jnp.float32),
+            pltpu.VMEM((here, group), jnp.bfloat16),
+            pltpu.VMEM((NY, group, rank), jnp.float32),
+            pltpu.VMEM((NY, group, rank // CORES), jnp.float32),
+            pltpu.VMEM((group, rank // CORES), jnp.float32),
+            pltpu.VMEM((NY, group, rank // CORES), jnp.bfloat16),
+            pltpu.VMEM((NY, group, rank // CORES), jnp.bfloat16),
+            pltpu.VMEM((nz, NY * slots, rank // CORES), jnp.bfloat16),
+            pltpu.VMEM((nz, NY * slots, rank // CORES), jnp.bfloat16),
+            pltpu.VMEM((here, rank // CORES), jnp.bfloat16),
+            pltpu.VMEM((NX, here, rank // CORES), jnp.bfloat16),
+            pltpu.VMEM((rank // CORES, lanes), jnp.float32),
+            pltpu.VMEM((part, lanes), jnp.float32),
             pltpu.VMEM((8, lanes), jnp.float32),
-            pltpu.VMEM((NX * CORES, 8, lanes), jnp.float32),
-            dma((3,)),
+            pltpu.VMEM((8, lanes), jnp.float32),
+            pltpu.VMEM((1, pattern.shape[1]), jnp.int32),
+            pltpu.VMEM((4, here), jnp.int32),
+            dma((5,)),
             dma((NY,)),
             dma((NY,)),
             dma((nz,)),
@@ -413,11 +438,11 @@
             dma((NY,)),
             dma((nz,)),
             dma((nz,)),
-            dma((NX * CORES,)),
-            dma((NX * CORES,)),
+            dma((2,)),
+            dma((2,)),
         ],
         compiler_params=pltpu.CompilerParams(
-            collective_id=0, has_side_effects=True, vmem_limit_bytes=48 * 1024 * 1024
+            collective_id=0, has_side_effects=True, vmem_limit_bytes=60 * 1024 * 1024
         ),
     )(
         fields.transpose(1, 0, 2),

time: 59.5 us -> 53.1 us (0.89)
  Pallas kernels: 54.3 us -> 49.7 us
  local copies, waits for them, and re-layouts: 3.83 us -> 1.37 us
  other arithmetic: 0.52 us -> 1.19 us
    pallas_call x1, Pallas kernels: 54.3 us -> 49.7 us  [per_device(): pl.pallas_call(functools.partial(kernel, sizes), out_shape=(jax.ShapeDtyp...]
    unnamed x9 -> x1, local copies, waits for them, and re-layouts: 3.83 us -> 1.37 us
    log1p x1, other arithmetic: 0.52 us -> 1.19 us  [per_device(): return (projection, jnp.log1p(energy.reshape(here) / rank))]
where the time goes in v2:
time: 53.1 us; the launch traced here: 52.9 us
  Pallas kernels  49.7 us (94%)
  local copies, waits for them, and re-layouts  1.37 us (3%)
  other arithmetic  1.19 us (2%)
  between operations  0.64 us (1%)
    pallas_call x1, Pallas kernels, per_device(): pl.pallas_call(functools.partial(kernel, sizes), out_shape=(jax.ShapeDtyp...  49.7 us
    unnamed x1, local copies, waits for them, and re-layouts  1.37 us
    log1p x1, other arithmetic, per_device(): return (projection, jnp.log1p(energy.reshape(here) / rank))  1.19 us

profile of v2, /device:TPU:1, one launch (start us, length us, event | category | flops | bytes accessed | tf_op | source)
XLA Modules:
  0.0 52.9 jit_solution(6223062931119229192)
XLA Ops:
  0.6 49.7 %shard_map.68 = (f32[64,64]{1,0:T(8,128)}, f32[1,64]{1,0:T(1,128)}) custom-call(bf16[3,16,8192]{2,1,0:T(8,128)(2,1)} %bitcast.5, f32[1,8192]{1,0:T(1,128)} %bitcast.6, bf16[8192,512]{1,0:T(8,128)(2,1)} %basis.1, s32[1,4]{1,0:T(1,128)} %pattern.1, s32[4,64]{1,0:T(4,128)} %bitcast.7), custom_call_target="tpu_custom_call" | custom-call | tf_op jit(solution)/shard_map/pallas_call | solution.py:394
  50.3 1.2 %log-plus-one_bitcast_fusion = f32[64]{0:T(128)} fusion(f32[1,64]{1,0:T(1,128)} %get-tuple-element.5), kind=kLoop, calls=%fused_computation | loop fusion | flops 64 | bytes 512 | tf_op jit(solution)/shard_map/log1p | solution.py:454
  51.5 1.4 %copy.8 = f32[64,64]{1,0:T(8,128)} copy(f32[64,64]{1,0:T(8,128)} %get-tuple-element.8) | data formatting | bytes 32768

commit v3 on v2

--- a/solution.py
+++ b/solution.py
@@ -27,6 +27,7 @@
     basis_here,
     weight_here,
     asked,
+    used,
     onehot,
     pick,
     partial,
@@ -45,6 +46,8 @@
     pattern_here,
     quads_here,
     local_sem,
+    use_send,
+    use_recv,
     ask_send,
     ask_y,
     ask_z_send,
@@ -64,7 +67,7 @@
     last_send,
     last_recv,
 ):
-    nz, block, cells, chunks, slots, rank, here = sizes
+    nz, block, cells, chunks, ahead, early, slots, rank, here = sizes
     quarter = cells // NY
     width = quarter // chunks
     lane_group = nz * NY * slots
@@ -118,11 +121,13 @@
         pl.semaphore_signal(barrier, inc=1, device_id=sibling, device_id_type=MESH)
         pads = (NY * 2 - 1) * block
         rows[:, pads:, :] = jnp.zeros((3, rows.shape[1] - pads, quarter), jnp.bfloat16)
-        asked[y, z] = jnp.full(asked.shape[2:], -1, jnp.int32)
         load_quads.wait()
         load_pattern.wait()
-        asked[y, z, 0:4, 0:here] = quads_here[...]
-        asked[y, z, 4:5, 0 : pattern.shape[1]] = pattern_here[...]
+        for pair in range(2):
+            asked[y, z, pair : pair + 1, 0:here] = quads_here[2 * pair : 2 * pair + 1, :]
+            asked[y, z, pair : pair + 1, here : 2 * here] = quads_here[2 * pair + 1 : 2 * pair + 2, :]
+        used[y] = jnp.zeros(used.shape[1:], jnp.int32)
+        used[y, 0:1, 0 : pattern.shape[1]] = pattern_here[...]
         pl.semaphore_wait(barrier, NY - 1 + nz - 1 + NX - 1 + CORES - 1)
 
     ask_copies = []
@@ -131,6 +136,10 @@
             remote(asked.at[y, z], asked.at[y, z], ask_send.at[d], ask_y.at[d], at_y(turn(y, d, NY)))
         )
         ask_copies[-1].start()
+    use_copies = []
+    for d in range(1, NY):
+        use_copies.append(remote(used.at[y], used.at[y], use_send.at[d], use_recv.at[d], at_y(turn(y, d, NY))))
+        use_copies[-1].start()
 
     def y_copy(c, d):
         target = turn(y, d, NY)
@@ -162,13 +171,16 @@
             above,
         )
 
-    for c in range(chunks):
+    def start_own(c):
+        @pl.when(y < NY - 1)
+        def _():
+            z_own(c).start()
+
         for d in (2, 1, 3):
             y_copy(c, d).start()
 
-        @pl.when(y < NY - 1)
-        def _(c=c):
-            z_own(c).start()
+    for c in range(ahead):
+        start_own(c)
 
     with jax.named_scope("ask"):
         for d in range(1, NY):
@@ -189,8 +201,12 @@
                 def _(c=c, source=source):
                     z_pass(c, source).start()
 
+            if c + ahead < chunks:
+                start_own(c + ahead)
+
     load_own.wait()
-    forward(0)
+    for c in range(early):
+        forward(c)
 
     lanes = asked.shape[-1]
     earlier = (
@@ -207,8 +223,13 @@
         devices = NY * nz
         group = NY * slots
 
+        first_half = lax.broadcasted_iota(jnp.int32, (devices, lanes), 1) < here
+
         def wide(row):
-            line = asked[:, :, row, :].reshape(devices, 1, lanes)
+            line = asked[:, :, row // 2, :].reshape(devices, lanes)
+            if row % 2:
+                line = pltpu.roll(line, lanes - here, 1)
+            line = jnp.where(first_half, line, -1).reshape(devices, 1, lanes)
             return jnp.broadcast_to(line, (devices, group, lanes))
 
         inner = lax.broadcasted_iota(jnp.int32, (devices, group, lanes), 1)
@@ -225,46 +246,54 @@
 
         a, b, m, n = (local(row).astype(jnp.int32) for row in range(4))
         offset = lax.shift_right_arithmetic(m - 1, 4) - lax.shift_right_arithmetic(a - 1, 4)
-        used = asked[:, z, 4, :].reshape(NY, 1, lanes)
-        used = jnp.broadcast_to(used, (NY, slots, lanes)).reshape(1, group, lanes)
-        used = jnp.broadcast_to(used, (devices, group, lanes)).reshape(half, lanes)
-        live = jnp.sum(jnp.where(lane == offset, used.astype(jnp.float32), 0.0), axis=1, keepdims=True)
+        for d in range(1, NY):
+            use_copies[d - 1].wait_recv()
+        tiles = used[:, 0, :].reshape(NY, 1, lanes)
+        tiles = jnp.broadcast_to(tiles, (NY, slots, lanes)).reshape(1, group, lanes)
+        tiles = jnp.broadcast_to(tiles, (devices, group, lanes)).reshape(half, lanes)
+        live = jnp.sum(jnp.where(lane == offset, tiles.astype(jnp.float32), 0.0), axis=1, keepdims=True)
         one = jnp.where(lane == a - 1, 1.0, 0.0) - jnp.where(lane == b - 1, 1.0, 0.0)
-        onehot[0:half] = (live * one).astype(jnp.bfloat16)
+        onehot[0] = (live * one).astype(jnp.bfloat16).reshape(onehot.shape[1:])
         two = jnp.where(lane == m - 1, 1.0, 0.0) - jnp.where(lane == n - 1, 1.0, 0.0)
-        onehot[half : 2 * half] = two.astype(jnp.bfloat16)
+        onehot[1] = two.astype(jnp.bfloat16).reshape(onehot.shape[1:])
 
         slot_row = lax.broadcasted_iota(jnp.int32, (lane_group, lanes), 0)
-        own_a = jnp.broadcast_to(lax.shift_right_arithmetic(asked[y, z, 0:1, :], 4), (lane_group, lanes))
+        own_a = jnp.where(first_half[0:1], asked[y, z, 0:1, :], -1)
+        own_a = jnp.broadcast_to(lax.shift_right_arithmetic(own_a, 4), (lane_group, lanes))
         own_block = jnp.where(own_a == lax.div(slot_row, slots), 1.0, 0.0)
         own_match = slot_match(own_block, lax.rem(slot_row, slots)).astype(jnp.float32)
         pick[...] = own_match.T[:here].astype(jnp.bfloat16)
         load_basis.wait()
         load_weight.wait()
 
-    def compute(c):
+    def gather(c):
         with jax.named_scope("gather_fields"):
             for b in range(NY - 1):
                 z_pass(c, b).wait_recv()
+
+    def project(c, sources, sinks):
+        span = slice(c * width, (c + 1) * width)
+        total = None
+        for component in range(3):
+            field = rows[component, :, span]
+            left = jnp.dot(sources, field, preferred_element_type=jnp.float32)
+            right = jnp.dot(sinks, field, preferred_element_type=jnp.float32)
+            term = left * right
+            total = term if total is None else total + term
+        sensitivity = total * weight_here[:, span]
+        high = sensitivity.astype(jnp.bfloat16)
+        low = (sensitivity - high.astype(jnp.float32)).astype(jnp.bfloat16)
+        part = jnp.dot(high, basis_here[span, :], preferred_element_type=jnp.float32)
+        return part + jnp.dot(low, basis_here[span, :], preferred_element_type=jnp.float32)
+
+    for c in range(chunks - 1):
+        if c + early < chunks:
+            forward(c + early)
+        gather(c)
         with jax.named_scope("sensitivity"):
-            span = slice(c * width, (c + 1) * width)
-            total = None
-            for component in range(3):
-                picked = jnp.dot(onehot[...], rows[component, :, span], preferred_element_type=jnp.float32)
-                term = picked[:half] * picked[half:]
-                total = term if total is None else total + term
-            sensitivity = total * weight_here[:, span]
-            high = sensitivity.astype(jnp.bfloat16)
-            low = (sensitivity - high.astype(jnp.float32)).astype(jnp.bfloat16)
-            part = jnp.dot(high, basis_here[span, :], preferred_element_type=jnp.float32)
-            part = part + jnp.dot(low, basis_here[span, :], preferred_element_type=jnp.float32)
+            part = project(c, onehot[0].reshape(half, lanes), onehot[1].reshape(half, lanes))
             part = part.reshape(partial.shape)
             partial[...] = part if c == 0 else partial[...] + part
-
-    for c in range(chunks):
-        if c + 1 < chunks:
-            forward(c + 1)
-        compute(c)
 
     def own_half(other):
         return pl.ds(pl.multiple_of(other * (rank // CORES), 128), rank // CORES)
@@ -283,18 +312,27 @@
         target = turn(y, d, NY)
         return remote(to_y.at[target], from_y.at[d], y_send.at[d], y_recv.at[d], at_y(target))
 
-    with jax.named_scope("sum_core"):
-        for d in (2, 1, 3, 0):
+    def sum_cores(d):
+        target = turn(y, d, NY)
+        core_copy(d).wait_recv()
+        summed = partial[target, :, own_half(core)] + from_core[target]
+        if d:
+            to_y[target] = summed.astype(jnp.bfloat16)
+            y_sum_copy(d).start()
+        else:
+            own_sum[...] = summed
+
+    gather(chunks - 1)
+    before = None
+    for d in (2, 1, 3, 0):
+        with jax.named_scope("last_chunk"):
+            target = turn(y, d, NY)
+            partial[target] = partial[target] + project(chunks - 1, onehot[0, target], onehot[1, target])
             core_copy(d).start()
-        for d in (2, 1, 3, 0):
-            target = turn(y, d, NY)
-            core_copy(d).wait_recv()
-            summed = partial[target, :, own_half(core)] + from_core[target]
-            if d:
-                to_y[target] = summed.astype(jnp.bfloat16)
-                y_sum_copy(d).start()
-            else:
-                own_sum[...] = summed
+        if before is not None:
+            sum_cores(before)
+        before = d
+    sum_cores(before)
 
     with jax.named_scope("sum_y"):
         total = own_sum[...]
@@ -356,7 +394,7 @@
         energy[...] = (own_energy[...] + sibling_energy[...])[0:1, :here]
 
     with jax.named_scope("drain"):
-        for copy in ask_copies:
+        for copy in ask_copies + use_copies:
             copy.wait_send()
         for c in range(chunks):
             for d in range(1, NY):
@@ -375,7 +413,7 @@
             copy.wait_send()
 
 
-def per_device(fields, cell_weight, resolution_basis, pattern, quadrupoles, chunks=4):
+def per_device(fields, cell_weight, resolution_basis, pattern, quadrupoles, chunks=4, ahead=4, early=3):
     block, components, cells = fields.shape
     rank = resolution_basis.shape[1]
     here = quadrupoles.shape[0]
@@ -390,7 +428,7 @@
     dma = pltpu.SemaphoreType.DMA
     vmem = pl.BlockSpec(memory_space=pltpu.VMEM)
     anywhere = pl.BlockSpec(memory_space=pl.ANY)
-    sizes = (nz, block, cells, chunks, slots, rank, here)
+    sizes = (nz, block, cells, chunks, ahead, early, slots, rank, here)
     projection, energy = pl.pallas_call(
         functools.partial(kernel, sizes),
         out_shape=(
@@ -403,8 +441,9 @@
             pltpu.VMEM((components, held, quarter), jnp.bfloat16),
             pltpu.VMEM((quarter, rank), jnp.bfloat16),
             pltpu.VMEM((1, quarter), jnp.float32),
-            pltpu.VMEM((NY, nz, 8, lanes), jnp.int32),
-            pltpu.VMEM((2 * half, lanes), jnp.bfloat16),
+            pltpu.VMEM((NY, nz, 2, lanes), jnp.int32),
+            pltpu.VMEM((NY, 8, lanes), jnp.int32),
+            pltpu.VMEM((2, NY, group, lanes), jnp.bfloat16),
             pltpu.VMEM((here, group), jnp.bfloat16),
             pltpu.VMEM((NY, group, rank), jnp.float32),
             pltpu.VMEM((NY, group, rank // CORES), jnp.float32),
@@ -422,6 +461,8 @@
             pltpu.VMEM((1, pattern.shape[1]), jnp.int32),
             pltpu.VMEM((4, here), jnp.int32),
             dma((5,)),
+            dma((NY,)),
+            dma((NY,)),
             dma((NY,)),
             dma((NY,)),
             dma((nz,)),

time: 53.1 us -> 49.8 us (0.938)
  Pallas kernels: 49.7 us -> 46.4 us
    pallas_call x1, Pallas kernels: 49.7 us -> 46.4 us  [per_device(): pl.pallas_call(functools.partial(kernel, sizes), out_shape=(jax.ShapeDtyp...]
where the time goes in v3:
time: 49.8 us; the launch traced here: 49.6 us
  Pallas kernels  46.4 us (93%)
  local copies, waits for them, and re-layouts  1.37 us (3%)
  other arithmetic  1.19 us (2%)
  between operations  0.64 us (1%)
    pallas_call x1, Pallas kernels, per_device(): pl.pallas_call(functools.partial(kernel, sizes), out_shape=(jax.ShapeDtyp...  46.4 us
    unnamed x1, local copies, waits for them, and re-layouts  1.37 us
    log1p x1, other arithmetic, per_device(): return (projection, jnp.log1p(energy.reshape(here) / rank))  1.19 us

profile of v3, /device:TPU:1, one launch (start us, length us, event | category | flops | bytes accessed | tf_op | source)
XLA Modules:
  0.0 49.6 jit_solution(11842459754217238752)
XLA Ops:
  0.6 46.4 %shard_map.68 = (f32[64,64]{1,0:T(8,128)}, f32[1,64]{1,0:T(1,128)}) custom-call(bf16[3,16,8192]{2,1,0:T(8,128)(2,1)} %bitcast.5, f32[1,8192]{1,0:T(1,128)} %bitcast.6, bf16[8192,512]{1,0:T(8,128)(2,1)} %basis.1, s32[1,4]{1,0:T(1,128)} %pattern.1, s32[4,64]{1,0:T(4,128)} %bitcast.7), custom_call_target="tpu_custom_call" | custom-call | tf_op jit(solution)/shard_map/pallas_call | solution.py:432
  47.0 1.2 %log-plus-one_bitcast_fusion = f32[64]{0:T(128)} fusion(f32[1,64]{1,0:T(1,128)} %get-tuple-element.5), kind=kLoop, calls=%fused_computation | loop fusion | flops 64 | bytes 512 | tf_op jit(solution)/shard_map/log1p | solution.py:495
  48.2 1.4 %copy.8 = f32[64,64]{1,0:T(8,128)} copy(f32[64,64]{1,0:T(8,128)} %get-tuple-element.8) | data formatting | bytes 32768

commit v4 on v3

--- a/solution.py
+++ b/solution.py
@@ -99,7 +99,7 @@
     load_basis = pltpu.make_async_copy(basis.at[pl.ds(y * quarter, quarter)], basis_here, local_sem.at[0])
     load_weight = pltpu.make_async_copy(weight.at[:, pl.ds(y * quarter, quarter)], weight_here, local_sem.at[1])
     load_own = pltpu.make_async_copy(
-        fields.at[:, :, pl.ds(y * quarter, quarter)], rows.at[:, pl.ds(y * block, block), :], local_sem.at[2]
+        fields.at[:, :, pl.ds(y * quarter, quarter)], rows.at[:, pl.ds((1 + y) * block, block), :], local_sem.at[2]
     )
     load_quads = pltpu.make_async_copy(quads, quads_here, local_sem.at[3])
     load_pattern = pltpu.make_async_copy(pattern, pattern_here, local_sem.at[4])
@@ -145,36 +145,41 @@
         target = turn(y, d, NY)
         return remote(
             fields.at[:, :, pl.ds(target * quarter + c * width, width)],
-            rows.at[:, pl.ds(y * block, block), pl.ds(c * width, width)],
+            rows.at[:, pl.ds((1 + y) * block, block), pl.ds(c * width, width)],
             fy_send.at[c, d],
             fy_recv.at[c, d],
             at_y(target),
         )
 
-    above = at_z(turn(z, nz - 1, nz))
-
-    def z_own(c):
+    above, below = at_z(turn(z, nz - 1, nz)), at_z(turn(z, 1, nz))
+    passed = ((0, above, 1 + NY), (1, above, 2 + NY), (NY - 1, below, 0))
+
+    def z_own(c, k):
+        _, device, place = passed[k]
         return remote(
             fields.at[:, :, pl.ds(y * quarter + c * width, width)],
-            rows.at[:, pl.ds((NY + y) * block, block), pl.ds(c * width, width)],
-            fz_send.at[c, y],
-            fz_recv.at[c, y],
-            above,
+            rows.at[:, pl.ds(place * block, block), pl.ds(c * width, width)],
+            fz_send.at[c, k],
+            fz_recv.at[c, k],
+            device,
         )
 
-    def z_pass(c, b):
+    def z_pass(c, k):
+        b, device, place = passed[k]
         return remote(
-            rows.at[:, pl.ds(b * block, block), pl.ds(c * width, width)],
-            rows.at[:, pl.ds((NY + b) * block, block), pl.ds(c * width, width)],
-            fz_send.at[c, b],
-            fz_recv.at[c, b],
-            above,
+            rows.at[:, pl.ds((1 + b) * block, block), pl.ds(c * width, width)],
+            rows.at[:, pl.ds(place * block, block), pl.ds(c * width, width)],
+            fz_send.at[c, k],
+            fz_recv.at[c, k],
+            device,
         )
 
     def start_own(c):
-        @pl.when(y < NY - 1)
-        def _():
-            z_own(c).start()
+        for k, (b, _, _) in enumerate(passed):
+
+            @pl.when(y == b)
+            def _(k=k):
+                z_own(c, k).start()
 
         for d in (2, 1, 3):
             y_copy(c, d).start()
@@ -190,6 +195,10 @@
                 remote(asked.at[:, z], asked.at[:, z], ask_z_send.at[d], ask_z.at[d], at_z(turn(z, d, nz)))
             )
             ask_copies[-1].start()
+        for d in range(1, NY):
+            use_copies[d - 1].wait_recv()
+        use_copies.append(remote(used.at[NY - 1], used.at[NY], use_send.at[0], use_recv.at[0], below))
+        use_copies[-1].start()
 
     def forward(c):
         with jax.named_scope("forward"):
@@ -197,9 +206,11 @@
                 y_copy(c, d).wait_recv()
                 source = turn(y, NY - d, NY)
 
-                @pl.when(source < NY - 1)
-                def _(c=c, source=source):
-                    z_pass(c, source).start()
+                for k, (b, _, _) in enumerate(passed):
+
+                    @pl.when(source == b)
+                    def _(c=c, k=k):
+                        z_pass(c, k).start()
 
             if c + ahead < chunks:
                 start_own(c + ahead)
@@ -222,6 +233,11 @@
             ask_copies[NY - 1 + d - 1].wait_recv()
         devices = NY * nz
         group = NY * slots
+
+        blocks = NY * nz
+
+        def source_of(a):
+            return jnp.where(a < 0, -1, lax.rem(lax.shift_right_arithmetic(a, 4) + 1, blocks))
 
         first_half = lax.broadcasted_iota(jnp.int32, (devices, lanes), 1) < here
 
@@ -233,22 +249,23 @@
             return jnp.broadcast_to(line, (devices, group, lanes))
 
         inner = lax.broadcasted_iota(jnp.int32, (devices, group, lanes), 1)
-        a_wide = wide(0)
-        in_block = jnp.where(lax.shift_right_arithmetic(a_wide, 4) == z * NY + lax.div(inner, slots), 1.0, 0.0)
+        in_block = jnp.where(source_of(wide(0)) == z * NY + lax.div(inner, slots), 1.0, 0.0)
         in_block = in_block.reshape(half, lanes)
         slot = lax.rem(inner, slots).reshape(half, lanes)
         match = slot_match(in_block, slot)
         lane = lax.broadcasted_iota(jnp.int32, (half, lanes), 1)
 
         def local(row):
-            value = (wide(row) - (z * NY * block - 1)).reshape(half, lanes).astype(jnp.float32)
+            value = wide(row) - (z * NY - 1) * block
+            value = jnp.where(value >= blocks * block, value - blocks * block, value) + 1
+            value = value.reshape(half, lanes).astype(jnp.float32)
             return jnp.sum(jnp.where(match, value, 0.0), axis=1, keepdims=True)
 
         a, b, m, n = (local(row).astype(jnp.int32) for row in range(4))
         offset = lax.shift_right_arithmetic(m - 1, 4) - lax.shift_right_arithmetic(a - 1, 4)
-        for d in range(1, NY):
-            use_copies[d - 1].wait_recv()
-        tiles = used[:, 0, :].reshape(NY, 1, lanes)
+        use_copies[-1].wait_recv()
+        tiles = jnp.concatenate([used[NY, 0:1], used[0, 0:1], used[1, 0:1], used[2, 0:1]], axis=0)
+        tiles = tiles.reshape(NY, 1, lanes)
         tiles = jnp.broadcast_to(tiles, (NY, slots, lanes)).reshape(1, group, lanes)
         tiles = jnp.broadcast_to(tiles, (devices, group, lanes)).reshape(half, lanes)
         live = jnp.sum(jnp.where(lane == offset, tiles.astype(jnp.float32), 0.0), axis=1, keepdims=True)
@@ -259,7 +276,7 @@
 
         slot_row = lax.broadcasted_iota(jnp.int32, (lane_group, lanes), 0)
         own_a = jnp.where(first_half[0:1], asked[y, z, 0:1, :], -1)
-        own_a = jnp.broadcast_to(lax.shift_right_arithmetic(own_a, 4), (lane_group, lanes))
+        own_a = jnp.broadcast_to(source_of(own_a), (lane_group, lanes))
         own_block = jnp.where(own_a == lax.div(slot_row, slots), 1.0, 0.0)
         own_match = slot_match(own_block, lax.rem(slot_row, slots)).astype(jnp.float32)
         pick[...] = own_match.T[:here].astype(jnp.bfloat16)
@@ -268,8 +285,8 @@
 
     def gather(c):
         with jax.named_scope("gather_fields"):
-            for b in range(NY - 1):
-                z_pass(c, b).wait_recv()
+            for k in range(len(passed)):
+                z_pass(c, k).wait_recv()
 
     def project(c, sources, sinks):
         span = slice(c * width, (c + 1) * width)
@@ -399,8 +416,8 @@
         for c in range(chunks):
             for d in range(1, NY):
                 y_copy(c, d).wait_send()
-            for b in range(NY - 1):
-                z_pass(c, b).wait_send()
+            for k in range(len(passed)):
+                z_pass(c, k).wait_send()
         for d in range(NY):
             core_copy(d).wait_send()
         for d in range(1, NY):
@@ -442,7 +459,7 @@
             pltpu.VMEM((quarter, rank), jnp.bfloat16),
             pltpu.VMEM((1, quarter), jnp.float32),
             pltpu.VMEM((NY, nz, 2, lanes), jnp.int32),
-            pltpu.VMEM((NY, 8, lanes), jnp.int32),
+            pltpu.VMEM((NY + 1, 8, lanes), jnp.int32),
             pltpu.VMEM((2, NY, group, lanes), jnp.bfloat16),
             pltpu.VMEM((here, group), jnp.bfloat16),
             pltpu.VMEM((NY, group, rank), jnp.float32),

time: 49.8 us -> 48.3 us (0.970)
  Pallas kernels: 46.4 us -> 44.9 us
    pallas_call x1, Pallas kernels: 46.4 us -> 44.9 us  [per_device(): pl.pallas_call(functools.partial(kernel, sizes), out_shape=(jax.ShapeDtyp...]
where the time goes in v4:
time: 48.3 us; the launch traced here: 48.1 us
  Pallas kernels  44.9 us (93%)
  local copies, waits for them, and re-layouts  1.37 us (3%)
  other arithmetic  1.19 us (2%)
  between operations  0.64 us (1%)
    pallas_call x1, Pallas kernels, per_device(): pl.pallas_call(functools.partial(kernel, sizes), out_shape=(jax.ShapeDtyp...  44.9 us
    unnamed x1, local copies, waits for them, and re-layouts  1.37 us
    log1p x1, other arithmetic, per_device(): return (projection, jnp.log1p(energy.reshape(here) / rank))  1.19 us

profile of v4, /device:TPU:1, one launch (start us, length us, event | category | flops | bytes accessed | tf_op | source)
XLA Modules:
  0.0 48.1 jit_solution(16123984696050791624)
XLA Ops:
  0.6 44.9 %shard_map.68 = (f32[64,64]{1,0:T(8,128)}, f32[1,64]{1,0:T(1,128)}) custom-call(bf16[3,16,8192]{2,1,0:T(8,128)(2,1)} %bitcast.5, f32[1,8192]{1,0:T(1,128)} %bitcast.6, bf16[8192,512]{1,0:T(8,128)(2,1)} %basis.1, s32[1,4]{1,0:T(1,128)} %pattern.1, s32[4,64]{1,0:T(4,128)} %bitcast.7), custom_call_target="tpu_custom_call" | custom-call | tf_op jit(solution)/shard_map/pallas_call | solution.py:449
  45.5 1.2 %log-plus-one_bitcast_fusion = f32[64]{0:T(128)} fusion(f32[1,64]{1,0:T(1,128)} %get-tuple-element.5), kind=kLoop, calls=%fused_computation | loop fusion | flops 64 | bytes 512 | tf_op jit(solution)/shard_map/log1p | solution.py:512
  46.7 1.4 %copy.8 = f32[64,64]{1,0:T(8,128)} copy(f32[64,64]{1,0:T(8,128)} %get-tuple-element.8) | data formatting | bytes 32768

commit v5 on v4

--- a/solution.py
+++ b/solution.py
@@ -26,6 +26,7 @@
     rows,
     basis_here,
     weight_here,
+    own_fields,
     asked,
     used,
     onehot,
@@ -67,9 +68,11 @@
     last_send,
     last_recv,
 ):
-    nz, block, cells, chunks, ahead, early, slots, rank, here = sizes
+    nz, block, cells, parts, ahead, early, slots, rank, here = sizes
     quarter = cells // NY
-    width = quarter // chunks
+    shares = [quarter * share // sum(parts) for share in parts]
+    chunks = len(parts)
+    starts = [sum(shares[:c]) for c in range(chunks)]
     lane_group = nz * NY * slots
     half = NY * lane_group
     elec = lax.axis_index("elec")
@@ -105,6 +108,8 @@
     load_pattern = pltpu.make_async_copy(pattern, pattern_here, local_sem.at[4])
     load_quads.start()
     load_pattern.start()
+    load_fields = pltpu.make_async_copy(fields, own_fields, local_sem.at[5])
+    load_fields.start()
     load_basis.start()
     load_weight.start()
     load_own.start()
@@ -128,6 +133,7 @@
             asked[y, z, pair : pair + 1, here : 2 * here] = quads_here[2 * pair + 1 : 2 * pair + 2, :]
         used[y] = jnp.zeros(used.shape[1:], jnp.int32)
         used[y, 0:1, 0 : pattern.shape[1]] = pattern_here[...]
+        load_fields.wait()
         pl.semaphore_wait(barrier, NY - 1 + nz - 1 + NX - 1 + CORES - 1)
 
     ask_copies = []
@@ -144,8 +150,8 @@
     def y_copy(c, d):
         target = turn(y, d, NY)
         return remote(
-            fields.at[:, :, pl.ds(target * quarter + c * width, width)],
-            rows.at[:, pl.ds((1 + y) * block, block), pl.ds(c * width, width)],
+            own_fields.at[:, :, pl.ds(target * quarter + starts[c], shares[c])],
+            rows.at[:, pl.ds((1 + y) * block, block), pl.ds(starts[c], shares[c])],
             fy_send.at[c, d],
             fy_recv.at[c, d],
             at_y(target),
@@ -157,8 +163,8 @@
     def z_own(c, k):
         _, device, place = passed[k]
         return remote(
-            fields.at[:, :, pl.ds(y * quarter + c * width, width)],
-            rows.at[:, pl.ds(place * block, block), pl.ds(c * width, width)],
+            own_fields.at[:, :, pl.ds(y * quarter + starts[c], shares[c])],
+            rows.at[:, pl.ds(place * block, block), pl.ds(starts[c], shares[c])],
             fz_send.at[c, k],
             fz_recv.at[c, k],
             device,
@@ -167,8 +173,8 @@
     def z_pass(c, k):
         b, device, place = passed[k]
         return remote(
-            rows.at[:, pl.ds((1 + b) * block, block), pl.ds(c * width, width)],
-            rows.at[:, pl.ds(place * block, block), pl.ds(c * width, width)],
+            rows.at[:, pl.ds((1 + b) * block, block), pl.ds(starts[c], shares[c])],
+            rows.at[:, pl.ds(place * block, block), pl.ds(starts[c], shares[c])],
             fz_send.at[c, k],
             fz_recv.at[c, k],
             device,
@@ -289,7 +295,7 @@
                 z_pass(c, k).wait_recv()
 
     def project(c, sources, sinks):
-        span = slice(c * width, (c + 1) * width)
+        span = slice(starts[c], starts[c] + shares[c])
         total = None
         for component in range(3):
             field = rows[component, :, span]
@@ -340,16 +346,13 @@
             own_sum[...] = summed
 
     gather(chunks - 1)
-    before = None
+    with jax.named_scope("last_chunk"):
+        part = project(chunks - 1, onehot[0].reshape(half, lanes), onehot[1].reshape(half, lanes))
+        partial[...] = partial[...] + part.reshape(partial.shape)
     for d in (2, 1, 3, 0):
-        with jax.named_scope("last_chunk"):
-            target = turn(y, d, NY)
-            partial[target] = partial[target] + project(chunks - 1, onehot[0, target], onehot[1, target])
-            core_copy(d).start()
-        if before is not None:
-            sum_cores(before)
-        before = d
-    sum_cores(before)
+        core_copy(d).start()
+    for d in (2, 1, 3, 0):
+        sum_cores(d)
 
     with jax.named_scope("sum_y"):
         total = own_sum[...]
@@ -430,8 +433,11 @@
             copy.wait_send()
 
 
-def per_device(fields, cell_weight, resolution_basis, pattern, quadrupoles, chunks=4, ahead=4, early=3):
+def per_device(fields, cell_weight, resolution_basis, pattern, quadrupoles):
     block, components, cells = fields.shape
+    parts = (1, 1, 1, 1)
+    chunks = ahead = len(parts)
+    early = chunks - 1
     rank = resolution_basis.shape[1]
     here = quadrupoles.shape[0]
     nz = lax.axis_size("elec") // NY
@@ -445,7 +451,7 @@
     dma = pltpu.SemaphoreType.DMA
     vmem = pl.BlockSpec(memory_space=pltpu.VMEM)
     anywhere = pl.BlockSpec(memory_space=pl.ANY)
-    sizes = (nz, block, cells, chunks, ahead, early, slots, rank, here)
+    sizes = (nz, block, cells, parts, ahead, early, slots, rank, here)
     projection, energy = pl.pallas_call(
         functools.partial(kernel, sizes),
         out_shape=(
@@ -458,6 +464,7 @@
             pltpu.VMEM((components, held, quarter), jnp.bfloat16),
             pltpu.VMEM((quarter, rank), jnp.bfloat16),
             pltpu.VMEM((1, quarter), jnp.float32),
+            pltpu.VMEM((components, block, cells), jnp.bfloat16),
             pltpu.VMEM((NY, nz, 2, lanes), jnp.int32),
             pltpu.VMEM((NY + 1, 8, lanes), jnp.int32),
             pltpu.VMEM((2, NY, group, lanes), jnp.bfloat16),
@@ -477,7 +484,7 @@
             pltpu.VMEM((8, lanes), jnp.float32),
             pltpu.VMEM((1, pattern.shape[1]), jnp.int32),
             pltpu.VMEM((4, here), jnp.int32),
-            dma((5,)),
+            dma((6,)),
             dma((NY,)),
             dma((NY,)),
             dma((NY,)),

time: 48.3 us -> 47.4 us (0.981)
  Pallas kernels: 44.9 us -> 44 us
    pallas_call x1, Pallas kernels: 44.9 us -> 44 us  [per_device(): pl.pallas_call(functools.partial(kernel, sizes), out_shape=(jax.ShapeDtyp...]
where the time goes in v5:
time: 47.4 us; the launch traced here: 47.2 us
  Pallas kernels  44 us (93%)
  local copies, waits for them, and re-layouts  1.37 us (3%)
  other arithmetic  1.19 us (3%)
  between operations  0.64 us (1%)
    pallas_call x1, Pallas kernels, per_device(): pl.pallas_call(functools.partial(kernel, sizes), out_shape=(jax.ShapeDtyp...  44 us
    unnamed x1, local copies, waits for them, and re-layouts  1.37 us
    log1p x1, other arithmetic, per_device(): return (projection, jnp.log1p(energy.reshape(here) / rank))  1.19 us

profile of v5, /device:TPU:1, one launch (start us, length us, event | category | flops | bytes accessed | tf_op | source)
XLA Modules:
  0.0 47.2 jit_solution(15385557385696242178)
XLA Ops:
  0.6 44.0 %shard_map.68 = (f32[64,64]{1,0:T(8,128)}, f32[1,64]{1,0:T(1,128)}) custom-call(bf16[3,16,8192]{2,1,0:T(8,128)(2,1)} %bitcast.5, f32[1,8192]{1,0:T(1,128)} %bitcast.6, bf16[8192,512]{1,0:T(8,128)(2,1)} %basis.1, s32[1,4]{1,0:T(1,128)} %pattern.1, s32[4,64]{1,0:T(4,128)} %bitcast.7), custom_call_target="tpu_custom_call" | custom-call | tf_op jit(solution)/shard_map/pallas_call | solution.py:455
  44.6 1.2 %log-plus-one_bitcast_fusion = f32[64]{0:T(128)} fusion(f32[1,64]{1,0:T(1,128)} %get-tuple-element.5), kind=kLoop, calls=%fused_computation | loop fusion | flops 64 | bytes 512 | tf_op jit(solution)/shard_map/log1p | solution.py:519
  45.8 1.4 %copy.8 = f32[64,64]{1,0:T(8,128)} copy(f32[64,64]{1,0:T(8,128)} %get-tuple-element.8) | data formatting | bytes 32768

commit v6 on v5

--- a/solution.py
+++ b/solution.py
@@ -379,17 +379,6 @@
         target = turn(x, d, NX)
         return remote(mine, from_x.at[d], x_send.at[d], x_recv.at[d], at_cell(target * CORES + core))
 
-    with jax.named_scope("sum_x"):
-        for d in (2, 1, 3):
-            x_copy(d).start()
-        total = mine[...].astype(jnp.float32)
-        for d in (1, 3, 2):
-            x_copy(d).wait_recv()
-            total = total + from_x[d].astype(jnp.float32)
-        total = jnp.concatenate([total, jnp.zeros((lanes - here, rank // CORES), jnp.float32)], axis=0).T
-        turned[...] = total
-        own_energy[...] = jnp.broadcast_to(jnp.sum(total * total, axis=0, keepdims=True), own_energy.shape)
-
     part = rank // (NX * CORES)
     chip_rows = lax.rem(x * CORES * part, rank // CORES)
     last = [
@@ -402,9 +391,20 @@
         ),
         remote(own_energy, sibling_energy, last_send.at[1], last_recv.at[1], sibling),
     ]
+    with jax.named_scope("sum_x"):
+        for d in (2, 1, 3):
+            x_copy(d).start()
+        total = mine[...].astype(jnp.float32)
+        for d in (1, 3, 2):
+            x_copy(d).wait_recv()
+            total = total + from_x[d].astype(jnp.float32)
+        total = jnp.concatenate([total, jnp.zeros((lanes - here, rank // CORES), jnp.float32)], axis=0).T
+        turned[...] = total
+        last[0].start()
+        own_energy[...] = jnp.broadcast_to(jnp.sum(total * total, axis=0, keepdims=True), own_energy.shape)
+
     with jax.named_scope("cores"):
-        for copy in last:
-            copy.start()
+        last[1].start()
         for copy in last:
             copy.wait_recv()
         kept = turned[pl.ds(pl.multiple_of(chip_rows + core * part, 8), part)]

time: 47.4 us -> 47.3 us (level)
  no operation moved by 1% of the time
where the time goes in v6:
time: 47.3 us; the launch traced here: 47.1 us
  Pallas kernels  43.9 us (93%)
  local copies, waits for them, and re-layouts  1.37 us (3%)
  other arithmetic  1.19 us (3%)
  between operations  0.64 us (1%)
    pallas_call x1, Pallas kernels, per_device(): pl.pallas_call(functools.partial(kernel, sizes), out_shape=(jax.ShapeDtyp...  43.9 us
    unnamed x1, local copies, waits for them, and re-layouts  1.37 us
    log1p x1, other arithmetic, per_device(): return (projection, jnp.log1p(energy.reshape(here) / rank))  1.19 us

profile of v6, /device:TPU:1, one launch (start us, length us, event | category | flops | bytes accessed | tf_op | source)
XLA Modules:
  0.0 47.1 jit_solution(14226606615981701770)
XLA Ops:
  0.6 43.9 %shard_map.68 = (f32[64,64]{1,0:T(8,128)}, f32[1,64]{1,0:T(1,128)}) custom-call(bf16[3,16,8192]{2,1,0:T(8,128)(2,1)} %bitcast.5, f32[1,8192]{1,0:T(1,128)} %bitcast.6, bf16[8192,512]{1,0:T(8,128)(2,1)} %basis.1, s32[1,4]{1,0:T(1,128)} %pattern.1, s32[4,64]{1,0:T(4,128)} %bitcast.7), custom_call_target="tpu_custom_call" | custom-call | tf_op jit(solution)/shard_map/pallas_call | solution.py:455
  44.6 1.2 %log-plus-one_bitcast_fusion = f32[64]{0:T(128)} fusion(f32[1,64]{1,0:T(1,128)} %get-tuple-element.5), kind=kLoop, calls=%fused_computation | loop fusion | flops 64 | bytes 512 | tf_op jit(solution)/shard_map/log1p | solution.py:519
  45.8 1.4 %copy.8 = f32[64,64]{1,0:T(8,128)} copy(f32[64,64]{1,0:T(8,128)} %get-tuple-element.8) | data formatting | bytes 32768
